TPU v7x, 32 devices: a whole 2x2x4 slice. The times are simulated.
32 devices in a mesh: tile: 8 (over z, y), lev: 4 (over x, core).
Axes of the slice: x: 2, y: 2, z: 4, core: 2. Of those that a mesh axis runs over, the one named last changes fastest.
Arguments:
- state: bfloat16 [4, 64, 512, 64], P(None, 'lev', 'tile'), may hold values from -6 to 6
- state_cotangent: bfloat16 [4, 64, 512, 64], P(None, 'lev', 'tile'), may hold values from -6 to 6
- diffusion: float32 [512, 64], P('tile'), may hold values from 0.05 to 0.24
- remap_weight: float32 [64, 4], replicated, may hold values from 0.05 to 0.5
- remap_band: int32 [64], replicated, may hold values from 0 to 60, as said below
- edge_table: int32 [8, 4, 4], P('tile'), may hold values from 0 to 7, as said below
- w_in: bfloat16 [1024, 256], replicated, may hold values from -0.375 to 0.375
- w_out: bfloat16 [256, 1024], replicated, may hold values from -0.1875 to 0.1875
Outputs:
- state_out: bfloat16 [4, 64, 512, 64], P(None, 'lev', 'tile')
- grad_state: bfloat16 [4, 64, 512, 64], P(None, 'lev', 'tile')
- grad_w_in: float32 [1024, 256], replicated
- grad_w_out: float32 [256, 1024], replicated
Inputs may be any that keep to these rules, and one draw needn't show every extreme that they name: `edge_table`: entry [t, e] describes edge e of tile t (0 first row, 1 last row, 2 first column, 3 last column): [t, e, 0] is the tile across it, [t, e, 1] that tile's matching edge, [t, e, 2] is 1 where the strip runs reversed and 0 else, [t, e, 3] the quarter turns 0 to 3 of the vector components. The matching is symmetric: the partner's entry points back, with the same reversal and the opposite turns modulo 4. The four edges of a tile meet four different tiles, none of them the tile itself. remap_band[k] lies between k - 2 and k + 1, clipped to the range; remap_band[0] is 0.
All inputs are finite; a program needn't handle non-finite values.
Results may differ from a plain program's by a relative error of at most 0.0075.
Values may be sent and summed in bfloat16 or wider, within the bound.
A program may use at most 128 MiB of HBM per device.

v0:
```python
import math

import jax
import jax.numpy as jnp
from jax import lax
from jax.sharding import PartitionSpec as P


def local_strips(block):
    return jnp.stack(
        [block[:, :, 0, :], block[:, :, -1, :], block[:, :, :, 0], block[:, :, :, -1]], axis=0
    )


def orient(strip, flipped, quarter):
    strip = jnp.where(flipped == 1, strip[..., ::-1], strip)
    cosine = (quarter == 0).astype(jnp.float32) - (quarter == 2).astype(jnp.float32)
    sine_part = (quarter == 1).astype(jnp.float32) - (quarter == 3).astype(jnp.float32)
    first = strip[0].astype(jnp.float32)
    second = strip[1].astype(jnp.float32)
    turned = jnp.stack(
        [cosine * first - sine_part * second, sine_part * first + cosine * second]
    ).astype(strip.dtype)
    return jnp.concatenate([turned, strip[2:]], axis=0)


def fetch_halo(block, table):
    strips = local_strips(block)
    targets = table[:, 0]
    sources = table[:, 1]
    piece = lax.all_gather(strips[None], "tile", axis=0, tiled=True)
    ranks = jnp.arange(piece.shape[0], dtype=jnp.int32)
    edge_ids = jnp.arange(4, dtype=jnp.int32)
    which = (
        (ranks[None, :, None] == targets[:, None, None])
        & (edge_ids[None, None, :] == sources[:, None, None])
    ).astype(jnp.bfloat16)
    picked = jnp.einsum("eqk,qkflc->eflc", which, piece, preferred_element_type=jnp.float32).astype(
        jnp.bfloat16
    )
    return jnp.stack([orient(picked[edge], table[edge, 2], table[edge, 3]) for edge in range(4)])


def neighbour_sum(block, halos):
    upper = jnp.concatenate([halos[0][:, :, None, :], block[:, :, :-1, :]], axis=2)
    lower = jnp.concatenate([block[:, :, 1:, :], halos[1][:, :, None, :]], axis=2)
    before = jnp.concatenate([halos[2][:, :, :, None], block[:, :, :, :-1]], axis=3)
    after = jnp.concatenate([block[:, :, :, 1:], halos[3][:, :, :, None]], axis=3)
    return upper + lower + before + after


def remap_matrix(weight, band):
    level_ids = jnp.arange(weight.shape[0], dtype=jnp.int32)
    matrix = jnp.zeros((weight.shape[0], weight.shape[0]), weight.dtype)
    for offset in range(weight.shape[1]):
        hits = (level_ids[None, :] == (band + offset)[:, None]).astype(weight.dtype)
        matrix = matrix + weight[:, offset][:, None] * hits
    return matrix


def band_remap(columns, weight, band):
    total = jnp.zeros(columns.shape, weight.dtype)
    for offset in range(weight.shape[1]):
        picked = jnp.take(columns, band + offset, axis=1).astype(weight.dtype)
        total = total + weight[:, offset][None, :, None] * picked
    return total.astype(jnp.bfloat16)


def contract(left, right, left_dim, right_dim):
    return lax.dot_general(
        left, right, (((left_dim,), (right_dim,)), ((), ())), preferred_element_type=jnp.float32
    )


def shards(state, state_cotangent, diffusion, remap_weight, remap_band, edge_table, w_in, w_out):
    tiles = lax.axis_size("tile")
    local_levels = state.shape[1]
    side = state.shape[3]
    levels = remap_weight.shape[0]
    features = w_in.shape[1]
    table = edge_table[0]
    values = state.astype(jnp.float32)
    halo = fetch_halo(state, table).astype(jnp.float32)
    moved = (values + diffusion * (neighbour_sum(values, halo) - 4.0 * values)).astype(jnp.bfloat16)
    flat_moved = moved.reshape(4, local_levels, side * side)
    flat_cotangent = state_cotangent.reshape(4, local_levels, side * side)
    whole = lax.all_to_all(flat_moved, "lev", split_axis=2, concat_axis=1, tiled=True)
    count = whole.shape[2]
    width = min(512, count)
    blocks = count // width
    remapped = band_remap(whole, remap_weight, remap_band)
    flat = remapped.reshape(features, count)

    def forward_block(index, output):
        cols = lax.dynamic_slice_in_dim(flat, index * width, width, 1)
        pre = jnp.dot(w_in, cols, preferred_element_type=jnp.float32)
        hidden = (pre * jax.nn.sigmoid(pre)).astype(jnp.bfloat16)
        result = (
            cols.astype(jnp.float32) + jnp.dot(w_out, hidden, preferred_element_type=jnp.float32)
        ).astype(jnp.bfloat16)
        return lax.dynamic_update_slice_in_dim(output, result, index * width, 1)

    output = lax.fori_loop(0, blocks, forward_block, jnp.zeros_like(flat))
    output = output.reshape(4, levels, count)
    state_back = lax.all_to_all(output, "lev", split_axis=1, concat_axis=2, tiled=True)
    grad_whole = lax.all_to_all(flat_cotangent, "lev", split_axis=2, concat_axis=1, tiled=True)
    grad_flat = grad_whole.reshape(features, count)

    def backward_block(index, carry):
        grad_in, grad_out, dflat = carry
        cols = lax.dynamic_slice_in_dim(flat, index * width, width, 1)
        grads = lax.dynamic_slice_in_dim(grad_flat, index * width, width, 1)
        pre = jnp.dot(w_in, cols, preferred_element_type=jnp.float32)
        sigma = jax.nn.sigmoid(pre)
        hidden = (pre * sigma).astype(jnp.bfloat16)
        back = contract(w_out, grads, 0, 0)
        slope = (sigma * (1.0 + pre * (1.0 - sigma)) * back).astype(jnp.bfloat16)
        grad_out = grad_out + contract(grads, hidden, 1, 1)
        grad_in = grad_in + contract(slope, cols, 1, 1)
        dcols = grads.astype(jnp.float32) + contract(w_in, slope, 0, 0)
        return (grad_in, grad_out, lax.dynamic_update_slice_in_dim(dflat, dcols, index * width, 1))

    start = (
        jnp.zeros(w_in.shape, jnp.float32),
        jnp.zeros(w_out.shape, jnp.float32),
        jnp.zeros((features, count), jnp.float32),
    )
    grad_in, grad_out, dflat = lax.fori_loop(0, blocks, backward_block, start)
    matrix = remap_matrix(remap_weight, remap_band)
    dmoved_cols = jnp.einsum(
        "kj,fkn->fjn", matrix, dflat.reshape(4, levels, count), precision=lax.Precision.HIGHEST
    ).astype(jnp.bfloat16)
    dmoved = lax.all_to_all(dmoved_cols, "lev", split_axis=1, concat_axis=2, tiled=True)
    grad_in, grad_out = lax.psum((grad_in, grad_out), ("tile", "lev"))
    dmoved = dmoved.reshape(4, local_levels, side, side)
    flux = (diffusion * dmoved.astype(jnp.float32)).astype(jnp.bfloat16)
    flux_halo = fetch_halo(flux, table).astype(jnp.float32)
    wide_flux = flux.astype(jnp.float32)
    grad_state = (
        dmoved.astype(jnp.float32) - 4.0 * wide_flux + neighbour_sum(wide_flux, flux_halo)
    ).astype(jnp.bfloat16)
    scale = 1.0 / math.sqrt(tiles * side * side)
    state_out = state_back.reshape(4, local_levels, side, side)
    return (state_out, grad_state, grad_in * scale, grad_out * scale)


def solution(mesh):
    placed = (
        P(None, "lev", "tile", None),
        P(None, "lev", "tile", None),
        P("tile", None),
        P(),
        P(),
        P("tile", None, None),
        P(),
        P(),
    )
    return jax.shard_map(
        shards,
        mesh=mesh,
        in_specs=placed,
        out_specs=(P(None, "lev", "tile", None), P(None, "lev", "tile", None), P(), P()),
        check_vma=False,
    )
```

profile of v0, /device:TPU:0, one launch (start us, length us, event | category | flops | bytes accessed | tf_op | source)
XLA Modules:
  0.0 324.5 jit_solution(15446711326868766442)
XLA Ops:
  7.2 1.0 fusion.101
  8.2 2.1 fusion.102
  21.7 2.6 fusion.99
  24.3 2.7 fusion.100
  28.0 33.0 %all-gather = bf16[32,4,16,64]{3,2,1,0:T(8,128)(2,1)S(1)} all-gather(bf16[4,4,16,64]{3,2,1,0:T(8,128)(2,1)S(1)} %pad_maximum_fusion), channel_id=2, replica_groups=mesh['tile'=8,'lev'=4] {'tile'}, dimensions={0}, use_global_device_ids=true | all-gather | bytes 294912 | tf_op jit(solution)/shard_map/all_gather | solution.py:31
  65.6 2.0 copy.300
  67.6 5.7 %fusion.28 = bf16[4,16,64,64]{3,2,1,0:T(8,128)(2,1)} fusion(f32[4,16,63,64]{3,2,1,0:T(8,128)} %get-tuple-element.457, f32[4,16,1,64]{3,2,1,0:T(1,128)S(1)} %bitcast.284, f32[4,16,1,64]{3,2,1,0:T(1,128)S(1)} %bitcast.283, f32[4,16,63,64]{3,2,1,0:T(8,128)} %get-tuple-element.456, f32[4,16,64,63]{3,2,1,0:T(8,128)} %get-tuple-element.455, ...), kind=kLoop, calls=%fused_computation.46 | loop fusion | flops 3407872 | bytes 5259264 | tf_op jit(solution)/shard_map/convert_element_type | solution.py:84
  73.3 7.3 %copy.332 = bf16[4,16,64,64]{1,0,3,2:T(4,128)(2,1)} copy(bf16[4,16,64,64]{3,2,1,0:T(8,128)(2,1)} %fusion.28) | data formatting | bytes 1048576 | tf_op jit(solution)/shard_map/reshape | solution.py:85
  80.7 6.5 %reshape.228 = bf16[4,2,32768]{2,1,0:T(2,128)(2,1)} reshape(bf16[4096,4,16]{2,1,0:T(4,128)(2,1)} %bitcast.268) | data formatting | bytes 1048576
  87.2 3.5 %all-to-all-start = ((bf16[4,2,32768]{2,1,0:T(2,128)(2,1)}), bf16[4,2,32768]{2,1,0:T(2,128)(2,1)S(1)}, u32[]{:S(2)}, u32[]{:S(2)}) async-start(bf16[4,2,32768]{2,1,0:T(2,128)(2,1)} %reshape.228), calls=%async_computation | async-start | bytes 1048576 | tf_op jit(solution)/shard_map/all_to_all | solution.py:87
  90.7 4.9 %copy.317 = bf16[4,16,64,64]{1,0,3,2:T(4,128)(2,1)} copy(bf16[4,16,64,64]{3,2,1,0:T(8,128)(2,1)S(1)} %copy-done.10) | data formatting | bytes 1048576 | tf_op args[1]
  95.7 6.5 %reshape.230 = bf16[4,2,32768]{2,1,0:T(2,128)(2,1)} reshape(bf16[4096,4,16]{2,1,0:T(4,128)(2,1)} %bitcast.269) | data formatting | bytes 1048576
  102.1 3.7 %all-to-all-start.2 = ((bf16[4,2,32768]{2,1,0:T(2,128)(2,1)}), bf16[4,2,32768]{2,1,0:T(2,128)(2,1)S(1)}, u32[]{:S(2)}, u32[]{:S(2)}) async-start(bf16[4,2,32768]{2,1,0:T(2,128)(2,1)} %reshape.230), calls=%async_computation.2 | async-start | bytes 1048576 | tf_op jit(solution)/shard_map/all_to_all | solution.py:106
  105.9 4.1 %reshape.229 = bf16[4096,4,16]{2,1,0:T(4,128)(2,1)} reshape(bf16[4,2,32768]{2,1,0:T(2,128)(2,1)S(1)} %all-to-all-done) | data formatting | bytes 1048576
  110.0 5.5 %copy.303 = bf16[4,4,16,1024]{3,2,1,0:T(8,128)(2,1)S(1)} copy(bf16[4,4,16,1024]{2,0,3,1:T(4,128)(2,1)} %bitcast.270) | data formatting | bytes 1048576 | tf_op jit(solution)/shard_map/all_to_all | solution.py:87
  115.9 1.0 gather_fusion.2
  116.9 1.0 gather_fusion.3
  117.9 1.0 gather_fusion.1
  118.9 1.0 gather_fusion
  119.9 4.1 %reshape.231 = bf16[4096,4,16]{2,1,0:T(4,128)(2,1)} reshape(bf16[4,2,32768]{2,1,0:T(2,128)(2,1)S(1)} %all-to-all-done.2) | data formatting | bytes 1048576
  124.0 6.6 %copy.319 = bf16[4,4,16,1024]{3,2,1,0:T(8,128)(2,1)} copy(bf16[4,4,16,1024]{2,0,3,1:T(4,128)(2,1)} %bitcast.271) | data formatting | bytes 1048576 | tf_op jit(solution)/shard_map/all_to_all | solution.py:106
  130.6 0.9 add_convert_fusion
  131.5 1.1 broadcast.110.clone.1
  132.6 30.6 %while.32 = (s32[]{:T(128)}, f32[1024,256]{1,0:T(8,128)}, f32[256,1024]{1,0:T(8,128)}, f32[256,1024]{1,0:T(8,128)}, bf16[256,1024]{1,0:T(8,128)(2,1)S(1)}, /*ind...) while((s32[]{:T(128)}, f32[1024,256]{1,0:T(8,128)}, ...), condition=%wide.region_3.5_spmd.clone, body=%wide.region_2.4_spmd.clone.sunk | while | flops 1350828032 | bytes 32768392 | solution.py:128
  133.1 0.7 copy-done.9
  133.9 0.7 copy-done.5
  134.6 0.9 fusion.149
  135.5 1.1 copy.419
  136.6 2.3 fusion.150
  138.9 2.0 copy.420
  140.9 1.9 constant_dynamic-update-slice_fusion.5
  142.8 2.4 convolution_add_fusion.4
  145.3 1.8 convolution_add_fusion.5
  147.6 0.7 copy-done.9
  148.4 0.7 copy-done.5
  149.0 0.9 fusion.149
  150.0 1.1 copy.419
  151.0 2.3 fusion.150
  153.4 2.0 copy.420
  155.4 1.9 constant_dynamic-update-slice_fusion.5
  157.3 2.8 convolution_add_fusion.4
  160.1 3.1 convolution_add_fusion.5
  163.2 2.4 fusion.33
  165.6 1.2 copy.322
  166.8 3.5 %all-to-all-start.3 = ((bf16[4,64,1024]{2,0,1:T(4,128)(2,1)}), bf16[4,64,1024]{2,0,1:T(4,128)(2,1)S(1)}, u32[]{:S(2)}, u32[]{:S(2)}) async-start(bf16[4,64,1024]{2,0,1:T(4,128)(2,1)} %copy.322), calls=%async_computation.3 | async-start | bytes 1048576 | tf_op jit(solution)/shard_map/all_to_all | solution.py:133
  170.4 2.5 while.31
  170.6 0.9 fusion.137
  171.9 0.9 fusion.137
  172.9 1.2 copy.314
  174.1 5.0 %all-to-all-done.3 = bf16[4,64,1024]{2,0,1:T(4,128)(2,1)S(1)} async-done(((bf16[4,64,1024]{2,0,1:T(4,128)(2,1)}), bf16[4,64,1024]{2,0,1:T(4,128)(2,1)S(1)}, u32[]{:S(2)}, u32[]{:S(2)}) %all-to-all-start.3) | async-done | bytes 524320 | tf_op jit(solution)/shard_map/all_to_all | solution.py:133
  179.1 4.3 %all-to-all-start.1 = ((bf16[4,64,1024]{2,0,1:T(4,128)(2,1)}), bf16[4,64,1024]{2,0,1:T(4,128)(2,1)}, u32[]{:S(2)}, u32[]{:S(2)}) async-start(bf16[4,64,1024]{2,0,1:T(4,128)(2,1)} %copy.314), calls=%async_computation.1 | async-start | bytes 1048576 | tf_op jit(solution)/shard_map/all_to_all | solution.py:105
  183.9 0.8 reshape.172
  185.0 1.5 slice_reduce_fusion.1
  186.6 31.9 %all-gather.1 = bf16[32,4,16,64]{3,2,1,0:T(8,128)(2,1)S(1)} all-gather(bf16[4,4,16,64]{3,2,1,0:T(8,128)(2,1)S(1)} %pad_maximum_fusion.1), channel_id=3, replica_groups=mesh['tile'=8,'lev'=4] {'tile'}, dimensions={0}, use_global_device_ids=true | all-gather | bytes 294912 | tf_op jit(solution)/shard_map/all_gather | solution.py:31
  219.7 2.0 copy.327
  221.8 2.0 copy.328
  223.8 1.2 copy.315
  225.0 1.2 copy.316
  226.2 2.5 reshape.168
  230.0 1.0 copy-done.7
  231.6 2.7 fusion.32
  234.2 79.9 %all-reduce.3.cloned.1.call-done = (f32[1024,256]{1,0:T(8,128)}, f32[256,1024]{1,0:T(8,128)}) async-done(((f32[1024,256]{1,0:T(8,128)}, f32[256,1024]{1,0:T(8,128)}), (f32[1024,256]{1,0:T(8,128)}, f32[256,1024]{1,0:T(8,128)})) %all-reduce.3.cloned.1.call-update) | async-done | bytes 2097168 | tf_op jit(solution)/shard_map/psum | solution.py:134
  314.1 2.4 broadcast_multiply_fusion
  316.5 1.1 broadcast_multiply_fusion.1
  (145 shorter events, 9.7 us)
Async XLA Ops:
  8.2 2.1 copy-start.13
  8.2 13.5 %copy-start = (bf16[4,16,64,64]{3,2,1,0:T(8,128)(2,1)S(1)}, bf16[4,16,64,64]{3,2,1,0:T(8,128)(2,1)}, u32[]{:S(2)}) copy-start(bf16[4,16,64,64]{3,2,1,0:T(8,128)(2,1)} %param.14) | copy-start | bytes 1572868
  64.9 2.7 copy-start.12
  80.7 10.0 %copy-start.14 = (s32[64]{0:T(128)S(1)}, s32[64]{0:T(128)}, u32[]{:S(2)}) copy-start(s32[64]{0:T(128)} %param.18) | copy-start | bytes 772
  80.7 10.1 %copy-start.10 = (bf16[4,16,64,64]{3,2,1,0:T(8,128)(2,1)S(1)}, bf16[4,16,64,64]{3,2,1,0:T(8,128)(2,1)}, u32[]{:S(2)}) copy-start(bf16[4,16,64,64]{3,2,1,0:T(8,128)(2,1)} %param.15) | copy-start | bytes 1572868
  87.2 14.9 %all-to-all-start = ((bf16[4,2,32768]{2,1,0:T(2,128)(2,1)}), bf16[4,2,32768]{2,1,0:T(2,128)(2,1)S(1)}, u32[]{:S(2)}, u32[]{:S(2)}) async-start(bf16[4,2,32768]{2,1,0:T(2,128)(2,1)} %reshape.228), calls=%async_computation | async-start | bytes 1048576 | tf_op jit(solution)/shard_map/all_to_all | solution.py:87
  95.7 10.2 %copy-start.15 = (f32[64,4]{0,1:T(4,128)S(1)}, f32[64,4]{0,1:T(4,128)}, u32[]{:S(2)}) copy-start(f32[64,4]{0,1:T(4,128)} %param.17) | copy-start | bytes 3076
  102.1 17.8 %all-to-all-start.2 = ((bf16[4,2,32768]{2,1,0:T(2,128)(2,1)}), bf16[4,2,32768]{2,1,0:T(2,128)(2,1)S(1)}, u32[]{:S(2)}, u32[]{:S(2)}) async-start(bf16[4,2,32768]{2,1,0:T(2,128)(2,1)} %reshape.230), calls=%async_computation.2 | async-start | bytes 1048576 | tf_op jit(solution)/shard_map/all_to_all | solution.py:106
  130.6 2.0 copy-start.1
  132.6 1.3 copy-start.3
  132.6 1.2 copy-start.9
  132.6 2.0 copy-start.16
  133.9 0.7 copy-start.5
  140.9 4.3 %copy-start.6 = (bf16[256,512]{1,0:T(8,128)(2,1)S(1)}, bf16[256,512]{1,0:T(8,128)(2,1)}, u32[]{:S(2)}) copy-start(bf16[256,512]{1,0:T(8,128)(2,1)} %copy-done.5) | copy-start | bytes 786436 | tf_op jit(solution)/shard_map/while
  145.3 1.8 copy-start.2
  145.3 1.8 copy-start.4
  147.1 1.3 copy-start.3
  147.1 1.2 copy-start.9
  147.1 2.0 copy-start.16
  148.3 0.7 copy-start.5
  155.4 4.7 %copy-start.6 = (bf16[256,512]{1,0:T(8,128)(2,1)S(1)}, bf16[256,512]{1,0:T(8,128)(2,1)}, u32[]{:S(2)}) copy-start(bf16[256,512]{1,0:T(8,128)(2,1)} %copy-done.5) | copy-start | bytes 786436 | tf_op jit(solution)/shard_map/while
  160.1 3.1 copy-start.2
  160.1 3.1 copy-start.4
  163.2 7.2 %copy-start.17 = (bf16[256,1024]{1,0:T(8,128)(2,1)S(1)}, bf16[256,1024]{1,0:T(8,128)(2,1)}, u32[]{:S(2)}) copy-start(bf16[256,1024]{1,0:T(8,128)(2,1)} %get-tuple-element.673) | copy-start | bytes 1572868
  166.8 12.3 %all-to-all-start.3 = ((bf16[4,64,1024]{2,0,1:T(4,128)(2,1)}), bf16[4,64,1024]{2,0,1:T(4,128)(2,1)S(1)}, u32[]{:S(2)}, u32[]{:S(2)}) async-start(bf16[4,64,1024]{2,0,1:T(4,128)(2,1)} %copy.322), calls=%async_computation.3 | async-start | bytes 1048576 | tf_op jit(solution)/shard_map/all_to_all | solution.py:133
  170.3 143.8 %all-reduce.3.cloned.1.call-start = ((), (), s32[]{:S(2)}) async-start(), calls=%async_computation.4 | async-start | bytes 4194304 | tf_op jit(solution)/shard_map/psum | solution.py:134
  179.1 44.7 %all-to-all-start.1 = ((bf16[4,64,1024]{2,0,1:T(4,128)(2,1)}), bf16[4,64,1024]{2,0,1:T(4,128)(2,1)}, u32[]{:S(2)}, u32[]{:S(2)}) async-start(bf16[4,64,1024]{2,0,1:T(4,128)(2,1)} %copy.314), calls=%async_computation.1 | async-start | bytes 1048576 | tf_op jit(solution)/shard_map/all_to_all | solution.py:105
  229.4 1.6 copy-start.7
  229.4 2.2 copy-start.8
  314.1 2.4 copy-start.11
Sparse Core Ops, SparseCore 0:
  177.2 136.8 all-reduce.2
where the time goes:
time: 326 us; the launch traced here: 324 us
  local copies, waits for them, and re-layouts  95.6 us (29%)
  waiting for transfers between devices  84.9 us (26%)
  blocking collectives  64.9 us (20%)
  between operations  27.8 us (9%)
  matrix products  22.7 us (7%)
  starting transfers between devices  15 us (5%)
  other arithmetic  13.5 us (4%)
    psum x1, waiting for transfers between devices, shards(): grad_in, grad_out = lax.psum((grad_in, grad_out), ('tile', 'lev'))  79.9 us
    all_gather x2, blocking collectives, fetch_halo(): piece = lax.all_gather(strips[None], 'tile', axis=0, tiled=True)  64.9 us
    unnamed x39, local copies, waits for them, and re-layouts  28.8 us
    dot_general x8, matrix products, contract(): lax.dot_general(left, right, (((left_dim,), (right_dim,)), ((), ())), pre...  16.5 us
    dynamic_update_slice x4, local copies, waits for them, and re-layouts, backward_block(): lax.dynamic_update_slice_in_dim(dflat, dcols, index * width, 1)  7.91 us
    reshape x1, local copies, waits for them, and re-layouts, shards(): flat_moved = moved.reshape(4, local_levels, side * side)  7.34 us
    all_to_all x1, local copies, waits for them, and re-layouts, shards(): lax.all_to_all(flat_cotangent, 'lev', split_axis=2, concat_axis=1, tiled=...  6.56 us
  transfers between devices with their start and end apart: 5, of which 2 were waited for; matrix products, arithmetic and copies ran while one was open for 14% of the time, Pallas kernels for 0%

commit v1 on v0

v1 whole, which is shorter than its diff:
```python
import functools
import math

import jax
import jax.numpy as jnp
from jax import lax
from jax.experimental import pallas as pl
from jax.experimental.pallas import tpu as pltpu
from jax.sharding import PartitionSpec as P

F32 = jnp.float32
BF16 = jnp.bfloat16
MESH = pl.DeviceIdType.MESH


def dot(a, b, dims=((1,), (0,))):
    return lax.dot_general(a, b, (dims, ((), ())), preferred_element_type=F32)


def body(tiles, state, cot, dif, wcol, bcol, wrow, brow, src, turn, w_in, w_out,
         o_state, o_grad, o_gin, o_gout,
         rel, s_a, g_a, m_a, g_x, m_x, o_x, d_x, o_a, d_a, f_a, edge, strip1, strip2, pick,
         xs, hid, slo, w_out_t, w_in_t, maps, gb, gf, r1, s2, r2, s3, r3, ag,
         ga_s, ga_r, ma_s, ma_r, oa_s, oa_r, da_s, da_r, h1_s, h1_r, h2_s, h2_r,
         p1_s, p1_r, p2_s, p2_r, p3_s, p3_r, p4_s, p4_r, p5_s, p5_r):
    t = lax.axis_index("tile")
    lev = lax.axis_index("lev")
    xpos = lev // 2
    core = lev % 2
    chunk = 1024 // tiles
    scale = 1.0 / math.sqrt(tiles * 4096)

    barrier = pltpu.get_barrier_semaphore()
    for d in range(1, 4):
        pl.semaphore_signal(barrier, inc=1, device_id={"lev": (lev + d) % 4}, device_id_type=MESH)

    def greet(d, _):
        pl.semaphore_signal(barrier, inc=1, device_id={"tile": (t + d) % tiles}, device_id_type=MESH)
        return 0

    lax.fori_loop(1, tiles, greet, 0)

    def rcopy(s, d, ss, rs, i, dev):
        return pltpu.make_async_remote_copy(
            src_ref=s, dst_ref=d, send_sem=ss.at[i], recv_sem=rs.at[i], device_id=dev, device_id_type=MESH)

    def to_columns(a, x, ss, rs, d):
        peer = (lev + d) % 4
        return rcopy(a.at[pl.ds(peer * 8, 8)], x.at[:, :, lev], ss, rs, d - 1, {"lev": peer})

    def to_levels(x, a, ss, rs, d):
        peer = (lev + d) % 4
        return rcopy(x.at[:, :, peer], a.at[pl.ds(lev * 8, 8)], ss, rs, d - 1, {"lev": peer})

    def share(buf, ss, rs, d):
        return rcopy(buf.at[t], buf.at[t], ss, rs, d - 1, {"tile": (t + d) % tiles})

    def each_tile(make, act):
        def step(d, _):
            act(make(d))
            return 0

        lax.fori_loop(1, tiles, step, 0)

    def pack(ref, blocks):
        def step(i, _):
            v = ref[i].astype(F32)
            rel[pl.ds(pl.multiple_of(i * 32, 32), 32), :] = jnp.concatenate([v[:32], v[32:]], axis=1)
            return 0

        lax.fori_loop(0, 64, step, 0, unroll=8)
        for b in range(32):
            blocks[b] = rel[pl.ds(b, 64, stride=32), :].astype(BF16).reshape(4, 16, 128)

    def unpack(ref):
        def step(i, _):
            v = rel[pl.ds(pl.multiple_of(i * 32, 32), 32), :]
            ref[i] = jnp.concatenate([v[:, :64], v[:, 64:]], axis=0).astype(BF16)
            return 0

        lax.fori_loop(0, 64, step, 0, unroll=8)

    row = lax.broadcasted_iota(jnp.int32, (256, 128), 0)
    lane = lax.broadcasted_iota(jnp.int32, (256, 128), 1)
    e = row // 64
    p = row % 64
    side_cell = (p % 32) * 128 + (p // 32) * 64
    cell = jnp.where(e == 0, p, jnp.where(e == 1, 31 * 128 + 64 + p, jnp.where(e == 2, side_cell, side_cell + 63)))
    cell = cell - lane
    pack(state, s_a)
    for b in range(32):
        edge[b] = (cell == b * 128).astype(F32).astype(BF16)

    def find_strips(blocks, strips):
        def step(b, total):
            return total + dot(blocks[b].reshape(64, 128), edge[b], ((1,), (1,)))

        total = lax.fori_loop(0, 32, step, jnp.zeros((64, 256), F32), unroll=4)
        strips[t] = total.astype(BF16)

    find_strips(s_a, strip1)
    pl.semaphore_wait(barrier, tiles + 2)
    each_tile(functools.partial(share, strip1, h1_s, h1_r), lambda c: c.start())

    pack(cot, g_a)
    g_copies = [to_columns(g_a, g_x, ga_s, ga_r, d) for d in range(1, 4)]
    for c in g_copies:
        c.start()
    g_x[:, :, lev] = g_a[pl.ds(lev * 8, 8)]

    row2 = lax.broadcasted_iota(jnp.int32, (256, 256), 0)
    lane2 = lax.broadcasted_iota(jnp.int32, (256, 256), 1)
    wanted = src[...] - row2

    def pick_step(i, _):
        pick[i] = (wanted == i * 256).astype(F32).astype(BF16)
        return 0

    lax.fori_loop(0, tiles, pick_step, 0)
    m = jnp.zeros((256, 256), F32)
    mt = jnp.zeros((256, 256), F32)
    for b in range(4):
        m = m + jnp.where(lane2 == bcol[...] + b, wcol[:, b:b + 1], 0.0)
        mt = mt + jnp.where(row2 == brow[...] + b, wrow[b:b + 1, :], 0.0)
    m_hi = m.astype(BF16)
    mt_hi = mt.astype(BF16)
    maps[0] = m_hi
    maps[1] = (m - m_hi.astype(F32)).astype(BF16)
    maps[2] = mt_hi
    maps[3] = (mt - mt_hi.astype(F32)).astype(BF16)
    w_out_t[...] = w_out[...].T
    w_in_t[...] = w_in[...].T
    dd = jnp.concatenate([dif[:32, :], dif[32:, :]], axis=1)

    def halos(strips):
        def step(i, total):
            return total + dot(strips[i], pick[i])

        h = lax.fori_loop(0, tiles, step, jnp.zeros((64, 256), F32))
        c = turn[0:1, :]
        s = turn[1:2, :]
        u = h[:16]
        v = h[16:32]
        return jnp.concatenate([c * u - s * v, s * u + c * v, h[32:]], axis=0).astype(BF16)

    lane64 = lax.broadcasted_iota(jnp.int32, (64, 128), 1)

    def neighbours(blocks, h, b):
        def at(i):
            return blocks[i].astype(F32).reshape(64, 128)

        v = at(b)
        if b == 0:
            up = jnp.where(lane64 >= 64, pltpu.roll(at(31), 64, 1), 0.0)
        else:
            up = at(b - 1)
        if b == 31:
            down = jnp.where(lane64 < 64, pltpu.roll(at(0), 64, 1), 0.0)
        else:
            down = at(b + 1)
        before = jnp.where(lane64 % 64 == 0, 0.0, pltpu.roll(v, 1, 1))
        after = jnp.where(lane64 % 64 == 63, 0.0, pltpu.roll(v, 127, 1))
        return v, up + down + before + after + dot(h, edge[b])

    each_tile(functools.partial(share, strip1, h1_s, h1_r), lambda c: c.wait())
    h = halos(strip1)
    for b in range(32):
        v, around = neighbours(s_a, h, b)
        moved = v + dd[b:b + 1, :] * (around - 4.0 * v)
        m_a[b] = moved.astype(BF16).reshape(4, 16, 128)
    m_copies = [to_columns(m_a, m_x, ma_s, ma_r, d) for d in range(1, 4)]
    for c in m_copies:
        c.start()
    m_x[:, :, lev] = m_a[pl.ds(lev * 8, 8)]
    for c in g_copies:
        c.wait()
    for c in m_copies:
        c.wait()

    def columns(k, _):
        def pair(ref):
            return jnp.concatenate([ref[2 * k].reshape(256, 128), ref[2 * k + 1].reshape(256, 128)], axis=1)

        at = pl.ds(pl.multiple_of(k * 256, 256), 256)
        moved = pair(m_x)
        g = pair(g_x)
        x = (dot(maps[0], moved) + dot(maps[1], moved)).astype(BF16)
        xs[:, at] = x
        pre = dot(w_in[...], x)
        sigma = jax.nn.sigmoid(pre)
        hidden = (pre * sigma).astype(BF16)
        hid[:, at] = hidden
        slope = (sigma * (1.0 + pre * (1.0 - sigma)) * dot(w_out_t[...], g)).astype(BF16)
        slo[:, at] = slope
        out = (x.astype(F32) + dot(w_out[...], hidden)).astype(BF16)
        dx = g.astype(F32) + dot(w_in_t[...], slope)
        dx_hi = dx.astype(BF16)
        dx_lo = (dx - dx_hi.astype(F32)).astype(BF16)
        dm = (dot(maps[2], dx_hi) + dot(maps[2], dx_lo) + dot(maps[3], dx_hi)).astype(BF16)
        for half in range(2):
            cut = slice(half * 128, half * 128 + 128)
            o_x[2 * k + half] = out[:, cut].reshape(4, 4, 16, 128)
            d_x[2 * k + half] = dm[:, cut].reshape(4, 4, 16, 128)
        return 0

    lax.fori_loop(0, 4, columns, 0)
    d_copies = [to_levels(d_x, d_a, da_s, da_r, d) for d in range(1, 4)]
    for c in d_copies:
        c.start()
    d_a[pl.ds(lev * 8, 8)] = d_x[:, :, lev]

    g_all = jnp.concatenate([g_x[b].reshape(256, 128) for b in range(8)], axis=1)
    for q in range(4):
        gin = dot(slo[q * 256:(q + 1) * 256, :], xs[...], ((1,), (1,)))
        for i in range(2):
            part = gin[:, i * 128:(i + 1) * 128]
            gf[q, i * 256:(i + 1) * 256] = part
            gb[q, i * 256:(i + 1) * 256] = part.astype(BF16)
    for i in range(4):
        gout = dot(g_all, hid[i * 256:(i + 1) * 256, :], ((1,), (1,)))
        for q in range(4):
            for j in range(2):
                part = gout[q * 64:(q + 1) * 64, j * 128:(j + 1) * 128]
                base = 512 + (2 * i + j) * 64
                gf[q, base:base + 64] = part
                gb[q, base:base + 64] = part.astype(BF16)
    mate = {"lev": xpos * 2 + 1 - core}
    across = {"lev": (1 - xpos) * 2 + core}
    first = [rcopy(gb.at[2 * i + 1 - core], r1.at[i], p1_s, p1_r, i, mate) for i in range(2)]

    for c in d_copies:
        c.wait()
    for c in first:
        c.start()
    for b in range(32):
        f_a[b] = (dd[b:b + 1, :] * d_a[b].astype(F32).reshape(64, 128)).astype(BF16).reshape(4, 16, 128)
    find_strips(f_a, strip2)
    each_tile(functools.partial(share, strip2, h2_s, h2_r), lambda c: c.start())

    for c in first:
        c.wait()
    s2[...] = (gf[2 * (1 - xpos) + core] + r1[1 - xpos].astype(F32)).astype(BF16)
    second = rcopy(s2, r2, p2_s, p2_r, 0, across)
    second.start()
    o_copies = [to_levels(o_x, o_a, oa_s, oa_r, d) for d in range(1, 4)]
    for c in o_copies:
        c.start()
    o_a[pl.ds(lev * 8, 8)] = o_x[:, :, lev]

    second.wait()
    s3[...] = (gf[lev] + r1[xpos].astype(F32) + r2[...].astype(F32)).astype(BF16).reshape(tiles, chunk, 128)

    def spread(d):
        other = (t + d) % tiles
        return rcopy(s3.at[other], r3.at[t], p3_s, p3_r, d - 1, {"tile": other})

    each_tile(spread, lambda c: c.start())
    r3[t] = s3[t]

    each_tile(functools.partial(share, strip2, h2_s, h2_r), lambda c: c.wait())
    h = halos(strip2)
    for b in range(32):
        v, around = neighbours(f_a, h, b)
        dm = d_a[b].astype(F32).reshape(64, 128)
        rel[pl.ds(b, 64, stride=32), :] = dm - 4.0 * v + around
    each_tile(spread, lambda c: c.wait())

    def add(i, total):
        return total + r3[i].astype(F32)

    ag[lev, t] = lax.fori_loop(0, tiles, add, jnp.zeros((chunk, 128), F32)).astype(BF16)

    def collect(d):
        return rcopy(ag.at[lev, t], ag.at[lev, t], p4_s, p4_r, d - 1, {"tile": (t + d) % tiles})

    each_tile(collect, lambda c: c.start())
    unpack(o_grad)
    each_tile(collect, lambda c: c.wait())
    last_x = rcopy(ag.at[lev], ag.at[lev], p5_s, p5_r, 0, across)
    last_c = rcopy(ag.at[lev], ag.at[lev], p5_s, p5_r, 1, mate)
    last_x.start()
    last_c.start()
    for c in o_copies:
        c.wait()
    for b in range(32):
        rel[pl.ds(b, 64, stride=32), :] = o_a[b].astype(F32).reshape(64, 128)
    unpack(o_state)
    last_x.wait()
    far = (1 - xpos) * 2 + core
    relay = rcopy(ag.at[far], ag.at[far], p5_s, p5_r, 2, mate)
    relay.start()
    last_c.wait()
    relay.wait()
    for q in range(4):
        whole = ag[q].reshape(1024, 128).astype(F32) * scale
        for i in range(2):
            o_gin[q * 256:(q + 1) * 256, i * 128:(i + 1) * 128] = whole[i * 256:(i + 1) * 256]
        for i in range(8):
            o_gout[q * 64:(q + 1) * 64, i * 128:(i + 1) * 128] = whole[512 + i * 64:576 + i * 64]


def shards(state, state_cotangent, diffusion, remap_weight, remap_band, edge_table, w_in, w_out):
    tiles = lax.axis_size("tile")
    table = edge_table[0]
    place = jnp.arange(64, dtype=jnp.int32)[None, :]
    along = jnp.where(table[:, 2:3] == 1, 63 - place, place)
    src = (table[:, 0:1] * 256 + table[:, 1:2] * 64 + along).reshape(1, 256)
    quarter = jnp.broadcast_to(table[:, 3:4], (4, 64)).reshape(1, 256)
    cosine = (quarter == 0).astype(F32) - (quarter == 2).astype(F32)
    sine = (quarter == 1).astype(F32) - (quarter == 3).astype(F32)
    turn = jnp.concatenate([cosine, sine], axis=0)
    field = jnp.arange(4, dtype=jnp.int32)[:, None] * 64
    band = (field + remap_band[None, :]).reshape(256)
    weight = jnp.tile(remap_weight, (4, 1))
    vm = pltpu.VMEM
    dma = pltpu.SemaphoreType.DMA
    block = vm((32, 4, 16, 128), BF16)
    cols = vm((8, 4, 4, 16, 128), BF16)
    chunk = 1024 // tiles
    out = pl.pallas_call(
        functools.partial(body, tiles),
        out_shape=(
            jax.ShapeDtypeStruct((64, 64, 64), BF16),
            jax.ShapeDtypeStruct((64, 64, 64), BF16),
            jax.ShapeDtypeStruct((1024, 256), F32),
            jax.ShapeDtypeStruct((256, 1024), F32),
        ),
        in_specs=[pl.BlockSpec(memory_space=vm)] * 11,
        out_specs=[pl.BlockSpec(memory_space=vm)] * 4,
        scratch_shapes=[
            vm((2048, 128), F32), block, block, block, cols, cols, cols, cols, block, block, block,
            vm((32, 256, 128), BF16), vm((tiles, 64, 256), BF16), vm((tiles, 64, 256), BF16),
            vm((tiles, 256, 256), BF16),
            vm((256, 1024), BF16), vm((1024, 1024), BF16), vm((1024, 1024), BF16),
            vm((1024, 256), BF16), vm((256, 1024), BF16), vm((4, 256, 256), BF16),
            vm((4, 1024, 128), BF16), vm((4, 1024, 128), F32), vm((2, 1024, 128), BF16),
            vm((1024, 128), BF16), vm((1024, 128), BF16), vm((tiles, chunk, 128), BF16),
            vm((tiles, chunk, 128), BF16), vm((4, tiles, chunk, 128), BF16),
            dma((3,)), dma((3,)), dma((3,)), dma((3,)), dma((3,)), dma((3,)), dma((3,)), dma((3,)),
            dma((tiles - 1,)), dma((tiles - 1,)), dma((tiles - 1,)), dma((tiles - 1,)),
            dma((2,)), dma((2,)), dma((1,)), dma((1,)),
            dma((tiles - 1,)), dma((tiles - 1,)), dma((tiles - 1,)), dma((tiles - 1,)),
            dma((3,)), dma((3,)),
        ],
        compiler_params=pltpu.CompilerParams(
            collective_id=0, has_side_effects=True, vmem_limit_bytes=60 * 1024 * 1024),
    )(
        state.reshape(64, 64, 64), state_cotangent.reshape(64, 64, 64), diffusion,
        weight, band[:, None], weight.T, band[None, :], src, turn, w_in, w_out,
    )
    shape = state.shape
    return out[0].reshape(shape), out[1].reshape(shape), out[2], out[3]


def solution(mesh):
    placed = (
        P(None, "lev", "tile", None),
        P(None, "lev", "tile", None),
        P("tile", None),
        P(),
        P(),
        P("tile", None, None),
        P(),
        P(),
    )
    return jax.shard_map(
        shards,
        mesh=mesh,
        in_specs=placed,
        out_specs=(P(None, "lev", "tile", None), P(None, "lev", "tile", None), P(), P()),
        check_vma=False,
    )
```

time: 326 us -> 82.6 us (0.25)
  waiting for transfers between devices: 84.9 us -> 0 us
  local copies, waits for them, and re-layouts: 95.6 us -> 11.2 us
  Pallas kernels: 0 us -> 69.1 us
  blocking collectives: 64.9 us -> 0 us
  between operations: 27.8 us -> 0.68 us
  matrix products: 22.7 us -> 0 us
  starting transfers between devices: 15 us -> 0 us
  other arithmetic: 13.5 us -> 1.29 us
    psum x1 -> x0, waiting for transfers between devices: 79.9 us -> none  [shards(): grad_in, grad_out = lax.psum((grad_in, grad_out), ('tile', 'lev'))]
    pallas_call x0 -> x1, Pallas kernels: none -> 69.1 us  [shards(): pl.pallas_call(functools.partial(body, tiles), out_shape=(jax.ShapeDtypeS...]
    all_gather x2 -> x0, blocking collectives: 64.9 us -> none  [fetch_halo(): piece = lax.all_gather(strips[None], 'tile', axis=0, tiled=True)]
    dot_general x15 -> x0, matrix products: 22.7 us -> none  [the longest x8 16.5 us: contract(): lax.dot_general(left, right, (((left_dim,), (right_dim,)), ((), ())), pre...]
    unnamed x39 -> x18, local copies, waits for them, and re-layouts: 28.8 us -> 7.96 us
    all_to_all x4 -> x0, starting transfers between devices: 15 us -> none  [the longest x1 4.35 us: shards(): lax.all_to_all(output, 'lev', split_axis=1, concat_axis=2, tiled=True)]
    all_to_all x5 -> x0, local copies, waits for them, and re-layouts: 14.9 us -> none  [the longest x1 6.56 us: shards(): lax.all_to_all(flat_cotangent, 'lev', split_axis=2, concat_axis=1, tiled=...]
    slice x20 -> x0, local copies, waits for them, and re-layouts: 12.2 us -> none  [the longest x2 3.58 us: local_strips(): block[:, :, :, 0]]
  transfers between devices with their start and end apart: 5 -> 0, of which waited for: 2 -> 0; matrix products, arithmetic and copies ran while one was open for 14% -> 0% of each run, Pallas kernels for 0% -> 0%
where the time goes in v1:
time: 82.6 us; the launch traced here: 82.2 us
  Pallas kernels  69.1 us (84%)
  local copies, waits for them, and re-layouts  11.2 us (14%)
  other arithmetic  1.29 us (2%)
    pallas_call x1, Pallas kernels, shards(): pl.pallas_call(functools.partial(body, tiles), out_shape=(jax.ShapeDtypeS...  69.1 us
    unnamed x18, local copies, waits for them, and re-layouts  7.96 us

profile of v1, /device:TPU:0, one launch (start us, length us, event | category | flops | bytes accessed | tf_op | source)
XLA Modules:
  0.0 82.2 jit_solution(14575200683819885885)
XLA Ops:
  0.6 0.0 copy-start.4
  0.6 0.7 copy-done.4
  1.3 0.2 fusion
  1.5 0.2 add_reduce_fusion
  1.7 0.1 select_add_fusion
  1.8 0.6 add.65.src
  2.4 0.2 subtract_reduce_fusion.1
  2.6 0.0 copy-start.6
  2.6 0.7 copy-done.6
  3.2 0.1 broadcast_add_fusion
  3.3 0.7 add.60.brow
  4.0 0.1 broadcast_in_dim.40
  4.0 0.1 sub.51
  4.1 0.1 broadcast_in_dim.41
  4.2 0.1 sub.54
  4.3 0.0 copy-start.5
  4.3 0.6 pad_maximum_fusion.turn
  4.9 0.1 copy-done.5
  5.0 0.1 tile.10
  5.0 0.0 copy-start.3
  5.0 0.8 add.66.bcol
  5.8 0.0 copy-done.3
  5.8 0.8 copy.13.wcol
  6.6 69.1 %shard_map.111 = (bf16[64,64,64]{2,1,0:T(8,128)(2,1)}, bf16[64,64,64]{2,1,0:T(8,128)(2,1)}, f32[1024,256]{1,0:T(8,128)}, f32[256,1024]{1,0:T(8,128)}) custom-call(bf16[64,64,64]{2,1,0:T(8,128)(2,1)} %bitcast.8, bf16[64,64,64]{2,1,0:T(8,128)(2,1)} %bitcast.9, f32[64,64]{1,0:T(8,128)} %dif.1, f32[256,4]{1,0:T(8,128)} %copy.13.wcol, s32[256,1]{1,0:T(8,128)} %add.66.bcol, ...), custom_call_target="tpu_custom_call" | custom-call | tf_op jit(solution)/shard_map/pallas_call | solution.py:320
  75.7 0.0 copy-start.2
  75.7 2.4 %copy.19 = bf16[4,16,64,64]{3,2,1,0:T(8,128)(2,1)} copy(bf16[4,16,64,64]{3,2,1,0:T(8,128)(2,1)} %bitcast.11) | data formatting | bytes 1048576
  78.1 0.0 copy-done.2
  78.1 0.0 copy-start.1
  78.1 1.0 %copy.20 = bf16[4,16,64,64]{3,2,1,0:T(8,128)(2,1)} copy(bf16[4,16,64,64]{3,2,1,0:T(8,128)(2,1)S(1)} %bitcast.10) | data formatting | bytes 1048576
  79.0 0.6 copy-done.1
  79.7 0.0 copy-start
  79.7 1.0 %copy.21 = f32[1024,256]{1,0:T(8,128)} copy(f32[1024,256]{1,0:T(8,128)S(1)} %copy-done.1) | data formatting | bytes 2097152
  80.6 0.6 copy-done
  81.3 1.0 %copy.22 = f32[256,1024]{1,0:T(8,128)} copy(f32[256,1024]{1,0:T(8,128)S(1)} %copy-done) | data formatting | bytes 2097152
  (3 shorter events, 0.0 us)
Async XLA Ops:
  0.6 0.7 copy-start.4
  2.6 0.7 copy-start.6
  4.3 0.7 copy-start.5
  5.0 0.8 copy-start.3
  75.7 2.4 %copy-start.2 = (bf16[64,64,64]{2,1,0:T(8,128)(2,1)S(1)}, bf16[64,64,64]{2,1,0:T(8,128)(2,1)}, u32[]{:S(2)}) copy-start(bf16[64,64,64]{2,1,0:T(8,128)(2,1)} %get-tuple-element.9) | copy-start | bytes 1572868
  78.1 1.6 %copy-start.1 = (f32[1024,256]{1,0:T(8,128)S(1)}, f32[1024,256]{1,0:T(8,128)}, u32[]{:S(2)}) copy-start(f32[1024,256]{1,0:T(8,128)} %get-tuple-element.20) | copy-start | bytes 3145732
  79.7 1.6 %copy-start = (f32[256,1024]{1,0:T(8,128)S(1)}, f32[256,1024]{1,0:T(8,128)}, u32[]{:S(2)}) copy-start(f32[256,1024]{1,0:T(8,128)} %get-tuple-element.21) | copy-start | bytes 3145732

commit v2 on v1

v2 whole, which is shorter than its diff:
```python
import functools
import math

import jax
import jax.numpy as jnp
from jax import lax
from jax.experimental import pallas as pl
from jax.experimental.pallas import tpu as pltpu
from jax.sharding import PartitionSpec as P

F32 = jnp.float32
BF16 = jnp.bfloat16
MESH = pl.DeviceIdType.MESH


def dot(a, b, dims=((1,), (0,))):
    return lax.dot_general(a, b, (dims, ((), ())), preferred_element_type=F32)


def body(tiles, table, state, cot, dif, weight, band, w_in, w_out,
         o_state, o_grad, o_gin, o_gout,
         rel, s_a, g_a, m_a, g_x, m_x, o_x, d_x, o_a, d_a, f_a, edge, strip1, strip2, pick,
         xs, hid, slo, w_out_t, w_in_t, maps,
         gb_in, gf_in, gb_out, gf_out, r1_in, r1_out, s2, r2, s3_in, r3_in, s3_out, r3_out, x_own, x_got, ag_in, ag_out,
         ga_s, ga_r, ma_s, ma_r, oa_s, oa_r, da_s, da_r, h1_s, h1_r, h2_s, h2_r,
         p1_s, p1_r, p2_s, p2_r, p3_s, p3_r, p4_s, p4_r, p5_s, p5_r, p6_s, p6_r, p7_s, p7_r):
    t = lax.axis_index("tile")
    lev = lax.axis_index("lev")
    xpos = lev // 2
    core = lev % 2
    scale = 1.0 / math.sqrt(tiles * 4096)

    barrier = pltpu.get_barrier_semaphore()
    for d in range(1, 4):
        pl.semaphore_signal(barrier, inc=1, device_id={"lev": (lev + d) % 4}, device_id_type=MESH)

    def greet(d, _):
        pl.semaphore_signal(barrier, inc=1, device_id={"tile": (t + d) % tiles}, device_id_type=MESH)
        return 0

    lax.fori_loop(1, tiles, greet, 0)

    def rcopy(s, d, ss, rs, i, dev):
        return pltpu.make_async_remote_copy(
            src_ref=s, dst_ref=d, send_sem=ss.at[i], recv_sem=rs.at[i], device_id=dev, device_id_type=MESH)

    def to_columns(a, x, ss, rs, k, d):
        peer = (lev + d) % 4
        return rcopy(a.at[pl.ds(peer * 8 + 2 * k, 2)], x.at[pl.ds(2 * k, 2), :, lev], ss, rs, k * 3 + d - 1, {"lev": peer})

    def to_levels(x, a, ss, rs, k, d):
        peer = (lev + d) % 4
        return rcopy(x.at[pl.ds(2 * k, 2), :, peer], a.at[pl.ds(lev * 8 + 2 * k, 2)], ss, rs, k * 3 + d - 1, {"lev": peer})

    def share(buf, ss, rs, d):
        return rcopy(buf.at[t], buf.at[t], ss, rs, d - 1, {"tile": (t + d) % tiles})

    def each_tile(make, act):
        def step(d, _):
            act(make(d))
            return 0

        lax.fori_loop(1, tiles, step, 0)

    def pack(ref, blocks):
        def step(i, _):
            v = ref[i].astype(F32)
            rel[pl.ds(pl.multiple_of(i * 32, 32), 32), :] = jnp.concatenate([v[:32], v[32:]], axis=1)
            return 0

        lax.fori_loop(0, 64, step, 0, unroll=8)
        for b in range(32):
            blocks[b] = rel[pl.ds(b, 64, stride=32), :].astype(BF16).reshape(4, 16, 128)

    def unpack(ref):
        def step(i, _):
            v = rel[pl.ds(pl.multiple_of(i * 32, 32), 32), :]
            ref[i] = jnp.concatenate([v[:, :64], v[:, 64:]], axis=0).astype(BF16)
            return 0

        lax.fori_loop(0, 64, step, 0, unroll=8)

    row = lax.broadcasted_iota(jnp.int32, (256, 128), 0)
    lane = lax.broadcasted_iota(jnp.int32, (256, 128), 1)
    e = row // 64
    p = row % 64
    side_cell = (p % 32) * 128 + (p // 32) * 64
    cell = jnp.where(e == 0, p, jnp.where(e == 1, 31 * 128 + 64 + p, jnp.where(e == 2, side_cell, side_cell + 63)))
    cell = cell - lane
    pack(state, s_a)
    for b in range(32):
        edge[b] = (cell == b * 128).astype(F32).astype(BF16)

    def find_strips(blocks, strips):
        def step(b, total):
            return total + dot(blocks[b].reshape(64, 128), edge[b], ((1,), (1,)))

        total = lax.fori_loop(0, 32, step, jnp.zeros((64, 256), F32), unroll=4)
        strips[t] = total.astype(BF16)

    find_strips(s_a, strip1)
    pl.semaphore_wait(barrier, tiles + 2)
    each_tile(functools.partial(share, strip1, h1_s, h1_r), lambda c: c.start())

    pack(cot, g_a)
    g_copies = [to_columns(g_a, g_x, ga_s, ga_r, k, d) for k in range(4) for d in range(1, 4)]
    for c in g_copies:
        c.start()
    g_x[:, :, lev] = g_a[pl.ds(lev * 8, 8)]

    row2 = lax.broadcasted_iota(jnp.int32, (256, 256), 0)
    lane1 = lax.broadcasted_iota(jnp.int32, (1, 256), 1)
    place = lane1 % 64
    src = jnp.zeros((1, 256), jnp.int32)
    quarter = jnp.zeros((1, 256), jnp.int32)
    for i in range(4):
        found = table[0, i, 0] * 256 + table[0, i, 1] * 64 + place + table[0, i, 2] * (63 - 2 * place)
        src = jnp.where(lane1 // 64 == i, found, src)
        quarter = jnp.where(lane1 // 64 == i, jnp.zeros((1, 256), jnp.int32) + table[0, i, 3], quarter)
    cosine = (quarter == 0).astype(F32) - (quarter == 2).astype(F32)
    sine = (quarter == 1).astype(F32) - (quarter == 3).astype(F32)
    wanted = src - row2

    def pick_step(i, _):
        pick[i] = (wanted == i * 256).astype(F32).astype(BF16)
        return 0

    lax.fori_loop(0, tiles, pick_step, 0)
    bands = jnp.concatenate([band[...] + 64 * i for i in range(4)], axis=1)
    weights = jnp.concatenate([weight[...]] * 4, axis=1)
    mt = jnp.zeros((256, 256), F32)
    for b in range(4):
        mt = mt + jnp.where(row2 == bands + b, weights[b:b + 1, :], 0.0)
    m = mt.T
    m_hi = m.astype(BF16)
    mt_hi = mt.astype(BF16)
    maps[0] = m_hi
    maps[1] = (m - m_hi.astype(F32)).astype(BF16)
    maps[2] = mt_hi
    maps[3] = (mt - mt_hi.astype(F32)).astype(BF16)
    w_out_t[...] = w_out[...].T
    w_in_t[...] = w_in[...].T
    dd = jnp.concatenate([dif[:32, :], dif[32:, :]], axis=1)

    def halos(strips):
        def step(i, total):
            return total + dot(strips[i], pick[i])

        h = lax.fori_loop(0, tiles, step, jnp.zeros((64, 256), F32))
        c, s = cosine, sine
        u = h[:16]
        v = h[16:32]
        return jnp.concatenate([c * u - s * v, s * u + c * v, h[32:]], axis=0).astype(BF16)

    lane64 = lax.broadcasted_iota(jnp.int32, (64, 128), 1)

    def neighbours(blocks, h, b):
        def at(i):
            return blocks[i].astype(F32).reshape(64, 128)

        v = at(b)
        if b == 0:
            up = jnp.where(lane64 >= 64, pltpu.roll(at(31), 64, 1), 0.0)
        else:
            up = at(b - 1)
        if b == 31:
            down = jnp.where(lane64 < 64, pltpu.roll(at(0), 64, 1), 0.0)
        else:
            down = at(b + 1)
        before = jnp.where(lane64 % 64 == 0, 0.0, pltpu.roll(v, 1, 1))
        after = jnp.where(lane64 % 64 == 63, 0.0, pltpu.roll(v, 127, 1))
        return v, up + down + before + after + dot(h, edge[b])

    each_tile(functools.partial(share, strip1, h1_s, h1_r), lambda c: c.wait())
    h = halos(strip1)
    m_copies = []
    for k in range(4):
        for b in [8 * j + 2 * k + i for j in range(4) for i in range(2)]:
            v, around = neighbours(s_a, h, b)
            moved = v + dd[b:b + 1, :] * (around - 4.0 * v)
            m_a[b] = moved.astype(BF16).reshape(4, 16, 128)
        m_copies.append([to_columns(m_a, m_x, ma_s, ma_r, k, d) for d in range(1, 4)])
        for c in m_copies[k]:
            c.start()
    m_x[:, :, lev] = m_a[pl.ds(lev * 8, 8)]
    for c in g_copies:
        c.wait()

    def columns(k):
        def pair(ref):
            return jnp.concatenate([ref[2 * k].reshape(256, 128), ref[2 * k + 1].reshape(256, 128)], axis=1)

        at = slice(k * 256, k * 256 + 256)
        moved = pair(m_x)
        g = pair(g_x)
        x = (dot(maps[0], moved) + dot(maps[1], moved)).astype(BF16)
        xs[:, at] = x
        pre = dot(w_in[...], x)
        sigma = jax.nn.sigmoid(pre)
        hidden = (pre * sigma).astype(BF16)
        hid[:, at] = hidden
        slope = (sigma * (1.0 + pre * (1.0 - sigma)) * dot(w_out_t[...], g)).astype(BF16)
        slo[:, at] = slope
        out = (x.astype(F32) + dot(w_out[...], hidden)).astype(BF16)
        dx = g.astype(F32) + dot(w_in_t[...], slope)
        dx_hi = dx.astype(BF16)
        dx_lo = (dx - dx_hi.astype(F32)).astype(BF16)
        dm = (dot(maps[2], dx_hi) + dot(maps[2], dx_lo) + dot(maps[3], dx_hi)).astype(BF16)
        for half in range(2):
            cut = slice(half * 128, half * 128 + 128)
            o_x[2 * k + half] = out[:, cut].reshape(4, 4, 16, 128)
            d_x[2 * k + half] = dm[:, cut].reshape(4, 4, 16, 128)

    d_copies = []
    for k in range(4):
        for c in m_copies[k]:
            c.wait()
        columns(k)
        now = [to_levels(d_x, d_a, da_s, da_r, k, d) for d in range(1, 4)]
        for c in now:
            c.start()
        d_copies += now
    o_copies = [to_levels(o_x, o_a, oa_s, oa_r, k, d) for k in range(4) for d in range(1, 4)]
    for c in o_copies:
        c.start()

    mate = {"lev": xpos * 2 + 1 - core}
    across = {"lev": (1 - xpos) * 2 + core}
    g_all = jnp.concatenate([g_x[b].reshape(256, 128) for b in range(8)], axis=1)
    for i in range(4):
        gout = dot(g_all, hid[i * 256:(i + 1) * 256, :], ((1,), (1,)))
        for q in range(4):
            for j in range(2):
                part = gout[q * 64:(q + 1) * 64, j * 128:(j + 1) * 128]
                base = (2 * i + j) * 64
                gf_out[q, base:base + 64] = part
                gb_out[q, base:base + 64] = part.astype(BF16)
    first_out = [rcopy(gb_out.at[2 * i + 1 - core], r1_out.at[i], p1_s, p1_r, i, mate) for i in range(2)]
    for c in first_out:
        c.start()
    for q in range(4):
        gin = dot(slo[q * 256:(q + 1) * 256, :], xs[...], ((1,), (1,)))
        for i in range(2):
            part = gin[:, i * 128:(i + 1) * 128]
            gf_in[q, i * 256:(i + 1) * 256] = part
            gb_in[q, i * 256:(i + 1) * 256] = part.astype(BF16)
    first_in = [rcopy(gb_in.at[2 * i + 1 - core], r1_in.at[i], p1_s, p1_r, 2 + i, mate) for i in range(2)]
    for c in first_in:
        c.start()
    d_a[pl.ds(lev * 8, 8)] = d_x[:, :, lev]
    o_a[pl.ds(lev * 8, 8)] = o_x[:, :, lev]

    def spread(s3, r3, ss, rs, d):
        other = (t + d) % tiles
        return rcopy(s3.at[other], r3.at[t], ss, rs, d - 1, {"tile": other})

    def collect(ag, part, ss, rs, d):
        return rcopy(ag.at[part, t], ag.at[part, t], ss, rs, d - 1, {"tile": (t + d) % tiles})

    def added(r3):
        def add(i, total):
            return total + r3[i].astype(F32)

        return lax.fori_loop(0, tiles, add, jnp.zeros(r3.shape[1:], F32)).astype(BF16)

    for c in first_out:
        c.wait()
    both = jnp.concatenate([gf_out[2 * i + core] + r1_out[i].astype(F32) for i in range(2)], axis=0)
    s3_out[...] = both.astype(BF16).reshape(s3_out.shape)
    spread_out = functools.partial(spread, s3_out, r3_out, p3_s, p3_r)
    each_tile(spread_out, lambda c: c.start())
    r3_out[t] = s3_out[t]
    for c in first_in:
        c.wait()
    s2[...] = (gf_in[2 * (1 - xpos) + core] + r1_in[1 - xpos].astype(F32)).astype(BF16)
    second = rcopy(s2, r2, p2_s, p2_r, 0, across)
    second.start()

    for c in d_copies:
        c.wait()
    for b in range(32):
        f_a[b] = (dd[b:b + 1, :] * d_a[b].astype(F32).reshape(64, 128)).astype(BF16).reshape(4, 16, 128)
    find_strips(f_a, strip2)
    each_tile(functools.partial(share, strip2, h2_s, h2_r), lambda c: c.start())

    second.wait()
    s3_in[...] = (gf_in[lev] + r1_in[xpos].astype(F32) + r2[...].astype(F32)).astype(BF16).reshape(s3_in.shape)
    spread_in = functools.partial(spread, s3_in, r3_in, p6_s, p6_r)
    each_tile(spread_in, lambda c: c.start())
    r3_in[t] = s3_in[t]

    each_tile(spread_out, lambda c: c.wait())
    x_own[...] = added(r3_out)
    swap = rcopy(x_own, x_got, p2_s, p2_r, 1, across)
    swap.start()

    each_tile(functools.partial(share, strip2, h2_s, h2_r), lambda c: c.wait())
    h = halos(strip2)
    swap.wait()
    ag_out[core, t] = (x_own[...].astype(F32) + x_got[...].astype(F32)).astype(BF16)
    collect_out = functools.partial(collect, ag_out, core, p4_s, p4_r)
    each_tile(collect_out, lambda c: c.start())
    each_tile(spread_in, lambda c: c.wait())
    ag_in[lev, t] = added(r3_in)
    collect_in = functools.partial(collect, ag_in, lev, p7_s, p7_r)
    each_tile(collect_in, lambda c: c.start())

    for b in range(32):
        v, around = neighbours(f_a, h, b)
        dm = d_a[b].astype(F32).reshape(64, 128)
        rel[pl.ds(b, 64, stride=32), :] = dm - 4.0 * v + around
    unpack(o_grad)
    each_tile(collect_in, lambda c: c.wait())
    last_x = rcopy(ag_in.at[lev], ag_in.at[lev], p5_s, p5_r, 0, across)
    last_c = rcopy(ag_in.at[lev], ag_in.at[lev], p5_s, p5_r, 1, mate)
    last_x.start()
    last_c.start()
    each_tile(collect_out, lambda c: c.wait())
    last_o = rcopy(ag_out.at[core], ag_out.at[core], p5_s, p5_r, 3, mate)
    last_o.start()
    for c in o_copies:
        c.wait()
    for b in range(32):
        rel[pl.ds(b, 64, stride=32), :] = o_a[b].astype(F32).reshape(64, 128)
    unpack(o_state)
    last_x.wait()
    far = (1 - xpos) * 2 + core
    relay = rcopy(ag_in.at[far], ag_in.at[far], p5_s, p5_r, 2, mate)
    relay.start()
    last_o.wait()
    for half in range(2):
        whole = ag_out[half].reshape(1024, 128).astype(F32) * scale
        for k in range(2):
            q = 2 * k + half
            for i in range(8):
                base = k * 512 + i * 64
                o_gout[q * 64:(q + 1) * 64, i * 128:(i + 1) * 128] = whole[base:base + 64]
    last_c.wait()
    relay.wait()
    for q in range(4):
        whole = ag_in[q].reshape(512, 128).astype(F32) * scale
        for i in range(2):
            o_gin[q * 256:(q + 1) * 256, i * 128:(i + 1) * 128] = whole[i * 256:(i + 1) * 256]


def shards(state, state_cotangent, diffusion, remap_weight, remap_band, edge_table, w_in, w_out):
    tiles = lax.axis_size("tile")
    vm = pltpu.VMEM
    dma = pltpu.SemaphoreType.DMA
    block = vm((32, 4, 16, 128), BF16)
    cols = vm((8, 4, 4, 16, 128), BF16)
    some_in = vm((tiles, 512 // tiles, 128), BF16)
    some_out = vm((tiles, 1024 // tiles, 128), BF16)
    out = pl.pallas_call(
        functools.partial(body, tiles),
        out_shape=(
            jax.ShapeDtypeStruct((64, 64, 64), BF16),
            jax.ShapeDtypeStruct((64, 64, 64), BF16),
            jax.ShapeDtypeStruct((1024, 256), F32),
            jax.ShapeDtypeStruct((256, 1024), F32),
        ),
        in_specs=[pl.BlockSpec(memory_space=pltpu.SMEM)] + [pl.BlockSpec(memory_space=vm)] * 7,
        out_specs=[pl.BlockSpec(memory_space=vm)] * 4,
        scratch_shapes=[
            vm((2048, 128), F32), block, block, block, cols, cols, cols, cols, block, block, block,
            vm((32, 256, 128), BF16), vm((tiles, 64, 256), BF16), vm((tiles, 64, 256), BF16),
            vm((tiles, 256, 256), BF16),
            vm((256, 1024), BF16), vm((1024, 1024), BF16), vm((1024, 1024), BF16),
            vm((1024, 256), BF16), vm((256, 1024), BF16), vm((4, 256, 256), BF16),
            vm((4, 512, 128), BF16), vm((4, 512, 128), F32), vm((4, 512, 128), BF16), vm((4, 512, 128), F32),
            vm((2, 512, 128), BF16), vm((2, 512, 128), BF16), vm((512, 128), BF16), vm((512, 128), BF16),
            some_in, some_in, some_out, some_out,
            vm((1024 // tiles, 128), BF16), vm((1024 // tiles, 128), BF16),
            vm((4, tiles, 512 // tiles, 128), BF16), vm((2, tiles, 1024 // tiles, 128), BF16),
            *[dma((12,))] * 8, *[dma((tiles - 1,))] * 4, *[dma((4,))] * 2, *[dma((2,))] * 2,
            *[dma((tiles - 1,))] * 4, *[dma((4,))] * 2, *[dma((tiles - 1,))] * 4,
        ],
        compiler_params=pltpu.CompilerParams(
            collective_id=0, has_side_effects=True, vmem_limit_bytes=60 * 1024 * 1024),
    )(
        edge_table, state.reshape(64, 64, 64), state_cotangent.reshape(64, 64, 64), diffusion,
        remap_weight.T, remap_band[None, :], w_in, w_out,
    )
    shape = state.shape
    return out[0].reshape(shape), out[1].reshape(shape), out[2], out[3]


def solution(mesh):
    placed = (
        P(None, "lev", "tile", None),
        P(None, "lev", "tile", None),
        P("tile", None),
        P(),
        P(),
        P("tile", None, None),
        P(),
        P(),
    )
    return jax.shard_map(
        shards,
        mesh=mesh,
        in_specs=placed,
        out_specs=(P(None, "lev", "tile", None), P(None, "lev", "tile", None), P(), P()),
        check_vma=False,
    )
```

time: 82.6 us -> 70.3 us (0.85)
  Pallas kernels: 69.1 us -> 62.9 us
  local copies, waits for them, and re-layouts: 11.2 us -> 6.53 us
  other arithmetic: 1.29 us -> 0 us
    pallas_call x1, Pallas kernels: 69.1 us -> 62.9 us  [shards(): pl.pallas_call(functools.partial(body, tiles), out_shape=(jax.ShapeDtypeS...]
    add x3 -> x0, local copies, waits for them, and re-layouts: 2.07 us -> none  [the longest x2 1.44 us: shards(): band = (field + remap_band[None, :]).reshape(256)]
    unnamed x18 -> x10, local copies, waits for them, and re-layouts: 7.96 us -> 6.53 us
    another operation x3 -> x0, local copies, waits for them, and re-layouts: 0.89 us -> none  [shards(): weight = jnp.tile(remap_weight, (4, 1))]
where the time goes in v2:
time: 70.3 us; the launch traced here: 70.1 us
  Pallas kernels  62.9 us (89%)
  local copies, waits for them, and re-layouts  6.53 us (9%)
    pallas_call x1, Pallas kernels, shards(): pl.pallas_call(functools.partial(body, tiles), out_shape=(jax.ShapeDtypeS...  62.9 us
    unnamed x10, local copies, waits for them, and re-layouts  6.53 us

profile of v2, /device:TPU:0, one launch (start us, length us, event | category | flops | bytes accessed | tf_op | source)
XLA Modules:
  0.0 70.1 jit_solution(7985730274384737869)
XLA Ops:
  0.6 62.9 %shard_map.111 = (bf16[64,64,64]{2,1,0:T(8,128)(2,1)}, bf16[64,64,64]{2,1,0:T(8,128)(2,1)}, f32[1024,256]{1,0:T(8,128)}, f32[256,1024]{1,0:T(8,128)}) custom-call(s32[1,4,4]{2,1,0:T(4,128)} %table.1, bf16[64,64,64]{2,1,0:T(8,128)(2,1)} %bitcast.8, bf16[64,64,64]{2,1,0:T(8,128)(2,1)} %bitcast.9, f32[64,64]{1,0:T(8,128)} %dif.1, f32[4,64]{1,0:T(4,128)} %bitcast.10, ...), custom_call_target="tpu_custom_call" | custom-call | tf_op jit(solution)/shard_map/pallas_call | solution.py:354
  63.5 0.0 copy-start.2
  63.5 2.4 %copy.16 = bf16[4,16,64,64]{3,2,1,0:T(8,128)(2,1)} copy(bf16[4,16,64,64]{3,2,1,0:T(8,128)(2,1)} %bitcast.7) | data formatting | bytes 1048576
  65.9 0.0 copy-done.2
  65.9 0.0 copy-start.1
  65.9 1.0 %copy.17 = bf16[4,16,64,64]{3,2,1,0:T(8,128)(2,1)} copy(bf16[4,16,64,64]{3,2,1,0:T(8,128)(2,1)S(1)} %bitcast.6) | data formatting | bytes 1048576
  66.9 0.6 copy-done.1
  67.5 0.0 copy-start
  67.5 1.0 %copy.18 = f32[1024,256]{1,0:T(8,128)} copy(f32[1024,256]{1,0:T(8,128)S(1)} %copy-done.1) | data formatting | bytes 2097152
  68.5 0.6 copy-done
  69.1 1.0 %copy.19 = f32[256,1024]{1,0:T(8,128)} copy(f32[256,1024]{1,0:T(8,128)S(1)} %copy-done) | data formatting | bytes 2097152
Async XLA Ops:
  63.5 2.4 %copy-start.2 = (bf16[64,64,64]{2,1,0:T(8,128)(2,1)S(1)}, bf16[64,64,64]{2,1,0:T(8,128)(2,1)}, u32[]{:S(2)}) copy-start(bf16[64,64,64]{2,1,0:T(8,128)(2,1)} %get-tuple-element.9) | copy-start | bytes 1572868
  65.9 1.6 %copy-start.1 = (f32[1024,256]{1,0:T(8,128)S(1)}, f32[1024,256]{1,0:T(8,128)}, u32[]{:S(2)}) copy-start(f32[1024,256]{1,0:T(8,128)} %get-tuple-element.18) | copy-start | bytes 3145732
  67.5 1.6 %copy-start = (f32[256,1024]{1,0:T(8,128)S(1)}, f32[256,1024]{1,0:T(8,128)}, u32[]{:S(2)}) copy-start(f32[256,1024]{1,0:T(8,128)} %get-tuple-element.19) | copy-start | bytes 3145732

commit v3 on v2

--- a/solution.py
+++ b/solution.py
@@ -220,9 +220,6 @@
         for c in now:
             c.start()
         d_copies += now
-    o_copies = [to_levels(o_x, o_a, oa_s, oa_r, k, d) for k in range(4) for d in range(1, 4)]
-    for c in o_copies:
-        c.start()
 
     mate = {"lev": xpos * 2 + 1 - core}
     across = {"lev": (1 - xpos) * 2 + core}
@@ -275,6 +272,9 @@
     s2[...] = (gf_in[2 * (1 - xpos) + core] + r1_in[1 - xpos].astype(F32)).astype(BF16)
     second = rcopy(s2, r2, p2_s, p2_r, 0, across)
     second.start()
+    o_copies = [to_levels(o_x, o_a, oa_s, oa_r, k, d) for k in range(4) for d in range(1, 4)]
+    for c in o_copies:
+        c.start()
 
     for c in d_copies:
         c.wait()
@@ -309,12 +309,12 @@
         v, around = neighbours(f_a, h, b)
         dm = d_a[b].astype(F32).reshape(64, 128)
         rel[pl.ds(b, 64, stride=32), :] = dm - 4.0 * v + around
-    unpack(o_grad)
     each_tile(collect_in, lambda c: c.wait())
     last_x = rcopy(ag_in.at[lev], ag_in.at[lev], p5_s, p5_r, 0, across)
     last_c = rcopy(ag_in.at[lev], ag_in.at[lev], p5_s, p5_r, 1, mate)
     last_x.start()
     last_c.start()
+    unpack(o_grad)
     each_tile(collect_out, lambda c: c.wait())
     last_o = rcopy(ag_out.at[core], ag_out.at[core], p5_s, p5_r, 3, mate)
     last_o.start()

time: 70.3 us -> 70.4 us (level)
  no operation moved by 1% of the time
where the time goes in v3:
time: 70.4 us; the launch traced here: 70.1 us
  Pallas kernels  62.9 us (89%)
  local copies, waits for them, and re-layouts  6.53 us (9%)
    pallas_call x1, Pallas kernels, shards(): pl.pallas_call(functools.partial(body, tiles), out_shape=(jax.ShapeDtypeS...  62.9 us
    unnamed x10, local copies, waits for them, and re-layouts  6.53 us

profile of v3, /device:TPU:0, one launch (start us, length us, event | category | flops | bytes accessed | tf_op | source)
XLA Modules:
  0.0 70.1 jit_solution(7668314322697249889)
XLA Ops:
  0.6 62.9 %shard_map.111 = (bf16[64,64,64]{2,1,0:T(8,128)(2,1)}, bf16[64,64,64]{2,1,0:T(8,128)(2,1)}, f32[1024,256]{1,0:T(8,128)}, f32[256,1024]{1,0:T(8,128)}) custom-call(s32[1,4,4]{2,1,0:T(4,128)} %table.1, bf16[64,64,64]{2,1,0:T(8,128)(2,1)} %bitcast.8, bf16[64,64,64]{2,1,0:T(8,128)(2,1)} %bitcast.9, f32[64,64]{1,0:T(8,128)} %dif.1, f32[4,64]{1,0:T(4,128)} %bitcast.10, ...), custom_call_target="tpu_custom_call" | custom-call | tf_op jit(solution)/shard_map/pallas_call | solution.py:354
  63.6 0.0 copy-start.2
  63.6 2.4 %copy.16 = bf16[4,16,64,64]{3,2,1,0:T(8,128)(2,1)} copy(bf16[4,16,64,64]{3,2,1,0:T(8,128)(2,1)} %bitcast.7) | data formatting | bytes 1048576
  66.0 0.0 copy-done.2
  66.0 0.0 copy-start.1
  66.0 1.0 %copy.17 = bf16[4,16,64,64]{3,2,1,0:T(8,128)(2,1)} copy(bf16[4,16,64,64]{3,2,1,0:T(8,128)(2,1)S(1)} %bitcast.6) | data formatting | bytes 1048576
  66.9 0.6 copy-done.1
  67.6 0.0 copy-start
  67.6 1.0 %copy.18 = f32[1024,256]{1,0:T(8,128)} copy(f32[1024,256]{1,0:T(8,128)S(1)} %copy-done.1) | data formatting | bytes 2097152
  68.5 0.6 copy-done
  69.2 1.0 %copy.19 = f32[256,1024]{1,0:T(8,128)} copy(f32[256,1024]{1,0:T(8,128)S(1)} %copy-done) | data formatting | bytes 2097152
Async XLA Ops:
  63.6 2.4 %copy-start.2 = (bf16[64,64,64]{2,1,0:T(8,128)(2,1)S(1)}, bf16[64,64,64]{2,1,0:T(8,128)(2,1)}, u32[]{:S(2)}) copy-start(bf16[64,64,64]{2,1,0:T(8,128)(2,1)} %get-tuple-element.9) | copy-start | bytes 1572868
  66.0 1.6 %copy-start.1 = (f32[1024,256]{1,0:T(8,128)S(1)}, f32[1024,256]{1,0:T(8,128)}, u32[]{:S(2)}) copy-start(f32[1024,256]{1,0:T(8,128)} %get-tuple-element.18) | copy-start | bytes 3145732
  67.6 1.6 %copy-start = (f32[256,1024]{1,0:T(8,128)S(1)}, f32[256,1024]{1,0:T(8,128)}, u32[]{:S(2)}) copy-start(f32[256,1024]{1,0:T(8,128)} %get-tuple-element.19) | copy-start | bytes 3145732
